TPU v7x, 32 devices: a whole 2x2x4 slice. The times are simulated.
32 devices in a mesh: section: 4 (over y, x), space: 8 (over z, core).
Axes of the slice: x: 2, y: 2, z: 4, core: 2. Of those that a mesh axis runs over, the one named last changes fastest.
Arguments:
- encoder_inputs: bfloat16 [4, 1, 128, 32, 2, 64], P('section', None, None, 'space'), may hold values from -6 to 6
- upper_inputs: bfloat16 [4, 1, 128, 32, 2, 64], P('section', None, None, 'space'), may hold values from -6 to 6
- output_cotangent: bfloat16 [1, 128, 32, 2, 64], P(None, None, 'space'), may hold values from -6 to 6
- weights: bfloat16 [4, 4, 3, 128, 1152], P('section'), may hold values from -0.15625 to 0.15625
- biases: float32 [4, 4, 128], P('section'), may hold values from -3 to 3
Outputs:
- encoder_grad: bfloat16 [4, 1, 128, 32, 2, 64], P('section', None, None, 'space')
- upper_grad: bfloat16 [4, 1, 128, 32, 2, 64], P('section', None, None, 'space')
- weight_grad: float32 [4, 4, 3, 128, 1152], P('section')
- bias_grad: float32 [4, 4, 128], P('section')
All inputs are finite; a program needn't handle non-finite values.
Results may differ from a plain program's by a relative error of at most 0.018.
Values may be sent and summed in bfloat16 or wider, within the bound.
A program may use at most 64 MiB of HBM per device.

v0:
```python
import jax
import jax.numpy as jnp
from jax import lax
from jax.sharding import PartitionSpec as P


def with_halo(block, sides, width):
    for axis, dim in sides:
        count = lax.axis_size(axis)
        forward = [(i, i + 1) for i in range(count - 1)]
        backward = [(target, source) for source, target in forward]
        low = lax.ppermute(
            lax.slice_in_dim(block, block.shape[dim] - width, None, axis=dim), axis, forward
        )
        high = lax.ppermute(lax.slice_in_dim(block, 0, width, axis=dim), axis, backward)
        block = jnp.concatenate([low, block, high], axis=dim)
    return block


def passed_along(array, axis, by):
    size = lax.axis_size(axis)
    pairs = [(i, i + by) for i in range(size) if 0 <= i + by < size]
    return lax.ppermute(array, axis, pairs)


def build_patches(field):
    shape = field.shape
    padded = jnp.pad(field, ((0, 0), (0, 0), (1, 1), (1, 1)))
    return jnp.concatenate(
        [
            padded[:, :, lateral : lateral + shape[2], depth : depth + shape[3]]
            for lateral in range(3)
            for depth in range(3)
        ],
        axis=0,
    )


def convolve_rows(field, kernel):
    stacked = build_patches(field)
    count = field.shape[1] - 2
    total = jnp.einsum(
        "ok,kxyz->oxyz", kernel[0], stacked[:, 0:count], preferred_element_type=jnp.float32
    )
    for offset in range(1, 3):
        total = total + jnp.einsum(
            "ok,kxyz->oxyz",
            kernel[offset],
            stacked[:, offset : offset + count],
            preferred_element_type=jnp.float32,
        )
    return total


def kernel_gradient(field, grads):
    stacked = build_patches(field)
    count = grads.shape[1]
    return jnp.stack(
        [
            jnp.einsum(
                "oxyz,kxyz->ok",
                grads,
                stacked[:, offset : offset + count],
                preferred_element_type=jnp.float32,
            )
            for offset in range(3)
        ]
    )


def kernel_sum(fields, grads):
    total = kernel_gradient(fields[0], grads[0])
    return total


def flipped(kernel):
    width = kernel.shape[1]
    shaped = kernel.reshape(3, width, 3, 3, width)[::-1, :, ::-1, ::-1, :]
    return shaped.transpose(0, 4, 2, 3, 1).reshape(3, width, 9 * width)


def silu_slope(pre):
    logistic = jax.nn.sigmoid(pre)
    return logistic * (1.0 + pre * (1.0 - logistic))


def inside_rows(count, margin, rows, total_rows):
    position = lax.axis_index("space") * rows - margin + jnp.arange(count)
    return ((position >= 0) & (position < total_rows)).astype(jnp.float32)[:, None, None]


def pick(store, slot):
    return lax.dynamic_index_in_dim(store, slot, 0, keepdims=False)


def place(store, value, slot, valid):
    current = lax.dynamic_index_in_dim(store, slot, 0, keepdims=False)
    return lax.dynamic_update_index_in_dim(store, jnp.where(valid, value, current), slot, 0)


def forward_deep(widened, kernel_pair, bias_pair, wide_mask):
    rows = widened.shape[2] - 8
    first_pre = jnp.stack([convolve_rows(widened[0], kernel_pair[0])]) + bias_pair[0]
    first_act = (jax.nn.silu(first_pre) * wide_mask).astype(jnp.bfloat16)
    second_pre = jnp.stack([convolve_rows(first_act[0], kernel_pair[1])]) + bias_pair[1]
    return (first_pre[:, :, 2 : rows + 4], second_pre, first_act[:, :, 2 : rows + 4])


def backward_deep(cotangent, first_pre, second_pre, flips, band):
    cotangent_wide = with_halo(cotangent, (("space", 1),), 2)
    second_grad = (cotangent_wide.astype(jnp.float32) * silu_slope(second_pre)).astype(jnp.bfloat16)
    hidden_grad = convolve_rows(second_grad, flips[1])
    first_grad = (hidden_grad * silu_slope(first_pre) * band).astype(jnp.bfloat16)
    input_grad = convolve_rows(first_grad, flips[0]).astype(jnp.bfloat16)
    return (input_grad, second_grad[:, 2:-2], first_grad[:, 1:-1])


def on_device(encoder_inputs, upper_inputs, output_cotangent, weights, biases):
    sections = lax.axis_size("section")
    section = lax.axis_index("section")
    encoder_input = encoder_inputs[0]
    upper_input = upper_inputs[0]
    kernels = weights[0]
    bias_field = biases[0][:, :, None, None, None]
    micro = encoder_input.shape[0]
    rows = encoder_input.shape[2]
    total_rows = rows * lax.axis_size("space")
    wide_mask = inside_rows(rows + 6, 3, rows, total_rows)
    band = inside_rows(rows + 2, 1, rows, total_rows)
    encoder_wide = with_halo(encoder_input, (("space", 2),), 4)
    encoder_saved = forward_deep(encoder_wide, kernels[0:2], bias_field[0:2], wide_mask)
    encoder_field = encoder_wide[:, :, 3 : rows + 5]
    encoder_top = encoder_saved[1][:, :, 2 : rows + 2]
    encoder_out = lax.optimization_barrier(jax.nn.silu(encoder_top).astype(jnp.bfloat16))
    decoder_input = (encoder_out.astype(jnp.float32) + upper_input.astype(jnp.float32)).astype(
        jnp.bfloat16
    )
    decoder_wide = with_halo(decoder_input, (("space", 2),), 4)
    decoder_saved = forward_deep(decoder_wide, kernels[2:4], bias_field[2:4], wide_mask)
    decoder_field = decoder_wide[:, :, 3 : rows + 5]
    encoder_flips = (flipped(kernels[0]), flipped(kernels[1]))
    decoder_flips = (flipped(kernels[2]), flipped(kernels[3]))

    def block_back(cotangent, first_pre, second_pre, flips):
        result = backward_deep(cotangent, first_pre, second_pre, flips, band)
        return result

    def decoder_phase(index, down_in, stores):
        valid = (index >= 0) & (index < micro)
        slot = jnp.clip(index, 0, micro - 1)
        arriving = jnp.where(section == 0, pick(output_cotangent, slot), down_in)
        input_grad, second_grad, first_grad = block_back(
            arriving, pick(decoder_saved[0], slot), pick(decoder_saved[1], slot), decoder_flips
        )
        stores = (
            place(stores[0], input_grad, slot, valid),
            place(stores[1], second_grad, slot, valid),
            place(stores[2], first_grad, slot, valid),
        )
        return (passed_along(input_grad, "section", 1), stores)

    def encoder_phase(index, above_in, skip_store, stores):
        valid = (index >= 0) & (index < micro)
        slot = jnp.clip(index, 0, micro - 1)
        combined = lax.optimization_barrier(
            (pick(skip_store, slot).astype(jnp.float32) + above_in.astype(jnp.float32)).astype(
                jnp.bfloat16
            )
        )
        input_grad, second_grad, first_grad = block_back(
            combined, pick(encoder_saved[0], slot), pick(encoder_saved[1], slot), encoder_flips
        )
        stores = (
            place(stores[0], input_grad, slot, valid),
            place(stores[1], second_grad, slot, valid),
            place(stores[2], first_grad, slot, valid),
        )
        return (passed_along(input_grad, "section", -1), stores)

    zero_field = jnp.zeros(encoder_input.shape[1:], jnp.bfloat16)
    empty = jnp.zeros(encoder_input.shape, jnp.bfloat16)

    def decoder_loop(tick, carry):
        return decoder_phase(tick - section, carry[0], carry[1])

    decoder_carry = lax.fori_loop(
        0, micro + sections - 1, decoder_loop, (zero_field, (empty, empty, empty))
    )
    decoder_stores = decoder_carry[1]

    def encoder_loop(tick, carry):
        return encoder_phase(tick - (sections - 1 - section), carry[0], decoder_stores[0], carry[1])

    encoder_carry = lax.fori_loop(
        0, micro + sections - 1, encoder_loop, (zero_field, (empty, empty, empty))
    )
    encoder_stores = encoder_carry[1]
    weight_terms = jnp.stack(
        [
            kernel_sum(encoder_field, encoder_stores[2]),
            kernel_sum(encoder_saved[2], encoder_stores[1]),
            kernel_sum(decoder_field, decoder_stores[2]),
            kernel_sum(decoder_saved[2], decoder_stores[1]),
        ]
    )
    bias_terms = jnp.stack(
        [
            jnp.sum(grads.astype(jnp.float32), axis=(0, 2, 3, 4))
            for grads in (
                encoder_stores[2],
                encoder_stores[1],
                decoder_stores[2],
                decoder_stores[1],
            )
        ]
    )
    weight_total, bias_total = lax.psum((weight_terms, bias_terms), "space")
    return (encoder_stores[0][None], decoder_stores[0][None], weight_total[None], bias_total[None])


def solution(mesh):
    return jax.shard_map(
        on_device,
        mesh=mesh,
        in_specs=(
            P("section", None, None, "space", None, None),
            P("section", None, None, "space", None, None),
            P(None, None, "space", None, None),
            P("section", None, None, None, None),
            P("section", None, None),
        ),
        out_specs=(
            P("section", None, None, "space", None, None),
            P("section", None, None, "space", None, None),
            P("section", None, None, None, None),
            P("section", None, None),
        ),
        check_vma=False,
    )
```

profile of v0, /device:TPU:23, one launch (start us, length us, event | category | flops | bytes accessed | tf_op | source)
XLA Modules:
  0.0 433.1 jit_solution(7259264218397280819)
XLA Ops:
  7.2 3.8 collective-permute-start.6
  50.7 3.6 collective-permute-start.8
  72.3 96.2 %while.44 = (s32[]{:T(128)}, bf16[128,4,2,64]{0,3,2,1:T(8,128)(2,1)}, bf16[1,128,4,2,64]{1,4,3,2,0:T(8,128)(2,1)S(1)}, bf16[1,128,4,2,64]{1,4,3,2,0:T(8,128)(2,1...) while((s32[]{:T(128)}, ...), condition=%wide.region_1.2_spmd.clone, body=%wide.region_0.1_spmd.clone.sunk | while | flops 1135443968 | bytes 38863864 | solution.py:186
  76.3 3.2 collective-permute-start.1
  89.6 4.3 collective-permute-done.2
  96.2 4.2 collective-permute-start
  113.8 4.3 collective-permute-done.2
  120.3 4.2 collective-permute-start
  137.9 4.9 %collective-permute-done.2 = bf16[128,4,2,64]{0,3,2,1:T(8,128)(2,1)S(1)} collective-permute-done((bf16[128,4,2,64]{0,3,2,1:T(8,128)(2,1)S(1)}, bf16[128,4,2,64]{0,3,2,1:T(8,128)(2,1)S(1)}, u32[]{:S(2)}, u32[]{:S(2)}) %collective-permute-start.2) | collective-permute-done | bytes 131104 | tf_op jit(solution)/shard_map/while/body/eval_jaxpr/ppermute | solution.py:23
  145.1 4.0 collective-permute-start
  162.3 5.5 %collective-permute-done.2 = bf16[128,4,2,64]{0,3,2,1:T(8,128)(2,1)S(1)} collective-permute-done((bf16[128,4,2,64]{0,3,2,1:T(8,128)(2,1)S(1)}, bf16[128,4,2,64]{0,3,2,1:T(8,128)(2,1)S(1)}, u32[]{:S(2)}, u32[]{:S(2)}) %collective-permute-start.2) | collective-permute-done | bytes 131104 | tf_op jit(solution)/shard_map/while/body/eval_jaxpr/ppermute | solution.py:23
  169.2 81.9 %while.45 = (s32[]{:T(128)}, bf16[128,4,2,64]{0,3,2,1:T(8,128)(2,1)S(1)}, bf16[1,128,4,2,64]{1,4,3,2,0:T(8,128)(2,1)}, bf16[1,128,4,2,64]{1,4,3,2,0:T(8,128)(2,1...) while((s32[]{:T(128)}, ...), condition=%wide.region_3.4_spmd.clone, body=%wide.region_2.3_spmd.clone.sunk | while | flops 1135640576 | bytes 38339540 | solution.py:194
  169.3 4.0 collective-permute-start.3
  183.6 4.5 %collective-permute-start.5 = (bf16[128,4,2,64]{0,3,2,1:T(8,128)(2,1)S(1)}, bf16[128,4,2,64]{0,3,2,1:T(8,128)(2,1)S(1)}, u32[]{:S(2)}, u32[]{:S(2)}) collective-permute-start(bf16[128,4,2,64]{0,3,2,1:T(8,128)(2,1)S(1)} %fusion.402), channel_id=1, source_target_pairs={{8,0},{16,8},{24,16},{9,1},{17,9},{25,17},{10,2},{18,10},{26,18},{... | collective-permute-start | bytes 393224 | tf_op jit(solution)/shard_map/while/body/eval_jaxpr/ppermute | solution.py:23
  190.1 3.9 collective-permute-start.3
  204.4 4.1 collective-permute-start.5
  210.5 3.9 collective-permute-start.3
  224.8 4.1 collective-permute-start.5
  230.8 3.9 collective-permute-start.3
  245.1 4.1 collective-permute-start.5
  260.2 3.3 maximum_bitcast_fusion
  263.7 12.0 %psum.15 = f32[1,4,128]{2,1,0:T(4,128)} all-reduce(f32[1,4,128]{2,1,0:T(4,128)S(1)} %maximum_bitcast_fusion.5), channel_id=1, replica_groups=mesh['section'=4,'space'=8] {'space'}, use_global_device_ids=true, to_apply=%region_9.10 | all-reduce | flops 512 | bytes 4096 | tf_op jit(solution)/shard_map/psum | solution.py:217
  275.6 144.2 %all-reduce.14.cloned.1.call-done = f32[1,4,3,128,1152]{4,3,2,1,0:T(8,128)} async-done(((f32[1,4,3,128,1152]{4,3,2,1,0:T(8,128)}), f32[1,4,3,128,1152]{4,3,2,1,0:T(8,128)}) %all-reduce.14.cloned.1.call-update) | async-done | bytes 7077904 | tf_op jit(solution)/shard_map/psum | solution.py:217
  419.8 6.4 %copy.192 = f32[1,4,3,128,1152]{4,3,2,1,0:T(8,128)} copy(f32[1,4,3,128,1152]{4,3,2,1,0:T(8,128)} %all-reduce.14.cloned.1.call-done) | data formatting | bytes 14155776
  (526 shorter events, 175.6 us)
Async XLA Ops:
  7.2 412.7 %all-reduce.14.cloned.1.call-start = ((), (), s32[]{:S(2)}) async-start(), calls=%async_computation | async-start | bytes 14155776 | tf_op jit(solution)/shard_map/psum | solution.py:217
  7.2 33.4 %collective-permute-start.6 = (bf16[1,128,4,2,64]{1,4,3,2,0:T(8,128)(2,1)}, bf16[1,128,4,2,64]{1,4,3,2,0:T(8,128)(2,1)}, u32[]{:S(2)}, u32[]{:S(2)}) collective-permute-start(bf16[1,128,4,2,64]{1,4,3,2,0:T(8,128)(2,1)} %bitcast.610), channel_id=1, source_target_pairs={{0,1},{1,2},{2,3},{3,4},{4,5},{5,6},{6,7},{8,9},{9,10},{10,11},{11... | collective-permute-start | bytes 393224 | tf_op jit(solution)/shard_map/ppermute | solution.py:12
  11.0 29.6 %collective-permute-start.7 = (bf16[1,128,4,2,64]{1,4,3,2,0:T(8,128)(2,1)}, bf16[1,128,4,2,64]{1,4,3,2,0:T(8,128)(2,1)}, u32[]{:S(2)}, u32[]{:S(2)}) collective-permute-start(bf16[1,128,4,2,64]{1,4,3,2,0:T(8,128)(2,1)} %bitcast.611), channel_id=1, source_target_pairs={{1,0},{2,1},{3,2},{4,3},{5,4},{6,5},{7,6},{9,8},{10,9},{11,10},{12... | collective-permute-start | bytes 393224 | tf_op jit(solution)/shard_map/ppermute | solution.py:15
  50.7 8.7 %collective-permute-start.8 = (bf16[1,128,4,2,64]{1,4,3,2,0:T(8,128)(2,1)S(1)}, bf16[1,128,4,2,64]{1,4,3,2,0:T(8,128)(2,1)S(1)}, u32[]{:S(2)}, u32[]{:S(2)}) collective-permute-start(bf16[1,128,4,2,64]{1,4,3,2,0:T(8,128)(2,1)S(1)} %fusion.183), channel_id=1, source_target_pairs={{0,1},{1,2},{2,3},{3,4},{4,5},{5,6},{6,7},{8,9},{9,10},{10,11},{11... | collective-permute-start | bytes 393224 | tf_op jit(solution)/shard_map/ppermute | solution.py:12
  54.4 6.3 %collective-permute-start.9 = (bf16[1,128,4,2,64]{1,4,3,2,0:T(8,128)(2,1)S(1)}, bf16[1,128,4,2,64]{1,4,3,2,0:T(8,128)(2,1)S(1)}, u32[]{:S(2)}, u32[]{:S(2)}) collective-permute-start(bf16[1,128,4,2,64]{1,4,3,2,0:T(8,128)(2,1)S(1)} %fusion.183), channel_id=1, source_target_pairs={{1,0},{2,1},{3,2},{4,3},{5,4},{6,5},{7,6},{9,8},{10,9},{11,10},{12... | collective-permute-start | bytes 393224 | tf_op jit(solution)/shard_map/ppermute | solution.py:15
  73.9 5.9 %collective-permute-start = (bf16[128,2,2,64]{0,3,2,1:T(8,128)(2,1)}, bf16[128,2,2,64]{0,3,2,1:T(8,128)(2,1)}, u32[]{:S(2)}, u32[]{:S(2)}) collective-permute-start(bf16[128,2,2,64]{0,3,2,1:T(8,128)(2,1)} %get-tuple-element.983), channel_id=1, source_target_pairs={{1,0},{2,1},{3,2},{4,3},{5,4},{6,5},{7,6},{9,8},{10,9},{11,10},{12... | collective-permute-start | bytes 196616 | tf_op jit(solution)/shard_map/while/body/eval_jaxpr/ppermute | solution.py:15
  76.3 4.8 %collective-permute-start.1 = (bf16[128,2,2,64]{0,3,2,1:T(8,128)(2,1)}, bf16[128,2,2,64]{0,3,2,1:T(8,128)(2,1)}, u32[]{:S(2)}, u32[]{:S(2)}) collective-permute-start(bf16[128,2,2,64]{0,3,2,1:T(8,128)(2,1)} %get-tuple-element.984), channel_id=1, source_target_pairs={{0,1},{1,2},{2,3},{3,4},{4,5},{5,6},{6,7},{8,9},{9,10},{10,11},{11... | collective-permute-start | bytes 196616 | tf_op jit(solution)/shard_map/while/body/eval_jaxpr/ppermute | solution.py:12
  88.2 5.7 %collective-permute-start.2 = (bf16[128,4,2,64]{0,3,2,1:T(8,128)(2,1)S(1)}, bf16[128,4,2,64]{0,3,2,1:T(8,128)(2,1)S(1)}, u32[]{:S(2)}, u32[]{:S(2)}) collective-permute-start(bf16[128,4,2,64]{0,3,2,1:T(8,128)(2,1)S(1)} %fusion.365), channel_id=1, source_target_pairs={{0,8},{8,16},{16,24},{1,9},{9,17},{17,25},{2,10},{10,18},{18,26},{... | collective-permute-start | bytes 393224 | tf_op jit(solution)/shard_map/while/body/eval_jaxpr/ppermute | solution.py:23
  96.2 7.7 %collective-permute-start = (bf16[128,2,2,64]{0,3,2,1:T(8,128)(2,1)}, bf16[128,2,2,64]{0,3,2,1:T(8,128)(2,1)}, u32[]{:S(2)}, u32[]{:S(2)}) collective-permute-start(bf16[128,2,2,64]{0,3,2,1:T(8,128)(2,1)} %get-tuple-element.983), channel_id=1, source_target_pairs={{1,0},{2,1},{3,2},{4,3},{5,4},{6,5},{7,6},{9,8},{10,9},{11,10},{12... | collective-permute-start | bytes 196616 | tf_op jit(solution)/shard_map/while/body/eval_jaxpr/ppermute | solution.py:15
  100.5 4.7 %collective-permute-start.1 = (bf16[128,2,2,64]{0,3,2,1:T(8,128)(2,1)}, bf16[128,2,2,64]{0,3,2,1:T(8,128)(2,1)}, u32[]{:S(2)}, u32[]{:S(2)}) collective-permute-start(bf16[128,2,2,64]{0,3,2,1:T(8,128)(2,1)} %get-tuple-element.984), channel_id=1, source_target_pairs={{0,1},{1,2},{2,3},{3,4},{4,5},{5,6},{6,7},{8,9},{9,10},{10,11},{11... | collective-permute-start | bytes 196616 | tf_op jit(solution)/shard_map/while/body/eval_jaxpr/ppermute | solution.py:12
  112.3 5.7 %collective-permute-start.2 = (bf16[128,4,2,64]{0,3,2,1:T(8,128)(2,1)S(1)}, bf16[128,4,2,64]{0,3,2,1:T(8,128)(2,1)S(1)}, u32[]{:S(2)}, u32[]{:S(2)}) collective-permute-start(bf16[128,4,2,64]{0,3,2,1:T(8,128)(2,1)S(1)} %fusion.365), channel_id=1, source_target_pairs={{0,8},{8,16},{16,24},{1,9},{9,17},{17,25},{2,10},{10,18},{18,26},{... | collective-permute-start | bytes 393224 | tf_op jit(solution)/shard_map/while/body/eval_jaxpr/ppermute | solution.py:23
  120.3 7.7 %collective-permute-start = (bf16[128,2,2,64]{0,3,2,1:T(8,128)(2,1)}, bf16[128,2,2,64]{0,3,2,1:T(8,128)(2,1)}, u32[]{:S(2)}, u32[]{:S(2)}) collective-permute-start(bf16[128,2,2,64]{0,3,2,1:T(8,128)(2,1)} %get-tuple-element.983), channel_id=1, source_target_pairs={{1,0},{2,1},{3,2},{4,3},{5,4},{6,5},{7,6},{9,8},{10,9},{11,10},{12... | collective-permute-start | bytes 196616 | tf_op jit(solution)/shard_map/while/body/eval_jaxpr/ppermute | solution.py:15
  124.6 4.7 %collective-permute-start.1 = (bf16[128,2,2,64]{0,3,2,1:T(8,128)(2,1)}, bf16[128,2,2,64]{0,3,2,1:T(8,128)(2,1)}, u32[]{:S(2)}, u32[]{:S(2)}) collective-permute-start(bf16[128,2,2,64]{0,3,2,1:T(8,128)(2,1)} %get-tuple-element.984), channel_id=1, source_target_pairs={{0,1},{1,2},{2,3},{3,4},{4,5},{5,6},{6,7},{8,9},{9,10},{10,11},{11... | collective-permute-start | bytes 196616 | tf_op jit(solution)/shard_map/while/body/eval_jaxpr/ppermute | solution.py:12
  136.4 6.3 %collective-permute-start.2 = (bf16[128,4,2,64]{0,3,2,1:T(8,128)(2,1)S(1)}, bf16[128,4,2,64]{0,3,2,1:T(8,128)(2,1)S(1)}, u32[]{:S(2)}, u32[]{:S(2)}) collective-permute-start(bf16[128,4,2,64]{0,3,2,1:T(8,128)(2,1)S(1)} %fusion.365), channel_id=1, source_target_pairs={{0,8},{8,16},{16,24},{1,9},{9,17},{17,25},{2,10},{10,18},{18,26},{... | collective-permute-start | bytes 393224 | tf_op jit(solution)/shard_map/while/body/eval_jaxpr/ppermute | solution.py:23
  145.1 7.4 %collective-permute-start = (bf16[128,2,2,64]{0,3,2,1:T(8,128)(2,1)}, bf16[128,2,2,64]{0,3,2,1:T(8,128)(2,1)}, u32[]{:S(2)}, u32[]{:S(2)}) collective-permute-start(bf16[128,2,2,64]{0,3,2,1:T(8,128)(2,1)} %get-tuple-element.983), channel_id=1, source_target_pairs={{1,0},{2,1},{3,2},{4,3},{5,4},{6,5},{7,6},{9,8},{10,9},{11,10},{12... | collective-permute-start | bytes 196616 | tf_op jit(solution)/shard_map/while/body/eval_jaxpr/ppermute | solution.py:15
  160.9 6.9 %collective-permute-start.2 = (bf16[128,4,2,64]{0,3,2,1:T(8,128)(2,1)S(1)}, bf16[128,4,2,64]{0,3,2,1:T(8,128)(2,1)S(1)}, u32[]{:S(2)}, u32[]{:S(2)}) collective-permute-start(bf16[128,4,2,64]{0,3,2,1:T(8,128)(2,1)S(1)} %fusion.365), channel_id=1, source_target_pairs={{0,8},{8,16},{16,24},{1,9},{9,17},{17,25},{2,10},{10,18},{18,26},{... | collective-permute-start | bytes 393224 | tf_op jit(solution)/shard_map/while/body/eval_jaxpr/ppermute | solution.py:23
  169.3 7.1 %collective-permute-start.3 = (bf16[128,2,2,64]{0,3,2,1:T(8,128)(2,1)S(1)}, bf16[128,2,2,64]{0,3,2,1:T(8,128)(2,1)S(1)}, u32[]{:S(2)}, u32[]{:S(2)}) collective-permute-start(bf16[128,2,2,64]{0,3,2,1:T(8,128)(2,1)S(1)} %get-tuple-element.1001), channel_id=1, source_target_pairs={{1,0},{2,1},{3,2},{4,3},{5,4},{6,5},{7,6},{9,8},{10,9},{11,10},{12... | collective-permute-start | bytes 196616 | tf_op jit(solution)/shard_map/while/body/eval_jaxpr/ppermute | solution.py:15
  183.6 6.5 %collective-permute-start.5 = (bf16[128,4,2,64]{0,3,2,1:T(8,128)(2,1)S(1)}, bf16[128,4,2,64]{0,3,2,1:T(8,128)(2,1)S(1)}, u32[]{:S(2)}, u32[]{:S(2)}) collective-permute-start(bf16[128,4,2,64]{0,3,2,1:T(8,128)(2,1)S(1)} %fusion.402), channel_id=1, source_target_pairs={{8,0},{16,8},{24,16},{9,1},{17,9},{25,17},{10,2},{18,10},{26,18},{... | collective-permute-start | bytes 393224 | tf_op jit(solution)/shard_map/while/body/eval_jaxpr/ppermute | solution.py:23
  190.1 7.1 %collective-permute-start.3 = (bf16[128,2,2,64]{0,3,2,1:T(8,128)(2,1)S(1)}, bf16[128,2,2,64]{0,3,2,1:T(8,128)(2,1)S(1)}, u32[]{:S(2)}, u32[]{:S(2)}) collective-permute-start(bf16[128,2,2,64]{0,3,2,1:T(8,128)(2,1)S(1)} %get-tuple-element.1001), channel_id=1, source_target_pairs={{1,0},{2,1},{3,2},{4,3},{5,4},{6,5},{7,6},{9,8},{10,9},{11,10},{12... | collective-permute-start | bytes 196616 | tf_op jit(solution)/shard_map/while/body/eval_jaxpr/ppermute | solution.py:15
  204.4 6.0 %collective-permute-start.5 = (bf16[128,4,2,64]{0,3,2,1:T(8,128)(2,1)S(1)}, bf16[128,4,2,64]{0,3,2,1:T(8,128)(2,1)S(1)}, u32[]{:S(2)}, u32[]{:S(2)}) collective-permute-start(bf16[128,4,2,64]{0,3,2,1:T(8,128)(2,1)S(1)} %fusion.402), channel_id=1, source_target_pairs={{8,0},{16,8},{24,16},{9,1},{17,9},{25,17},{10,2},{18,10},{26,18},{... | collective-permute-start | bytes 393224 | tf_op jit(solution)/shard_map/while/body/eval_jaxpr/ppermute | solution.py:23
  210.5 7.1 %collective-permute-start.3 = (bf16[128,2,2,64]{0,3,2,1:T(8,128)(2,1)S(1)}, bf16[128,2,2,64]{0,3,2,1:T(8,128)(2,1)S(1)}, u32[]{:S(2)}, u32[]{:S(2)}) collective-permute-start(bf16[128,2,2,64]{0,3,2,1:T(8,128)(2,1)S(1)} %get-tuple-element.1001), channel_id=1, source_target_pairs={{1,0},{2,1},{3,2},{4,3},{5,4},{6,5},{7,6},{9,8},{10,9},{11,10},{12... | collective-permute-start | bytes 196616 | tf_op jit(solution)/shard_map/while/body/eval_jaxpr/ppermute | solution.py:15
  224.8 6.0 %collective-permute-start.5 = (bf16[128,4,2,64]{0,3,2,1:T(8,128)(2,1)S(1)}, bf16[128,4,2,64]{0,3,2,1:T(8,128)(2,1)S(1)}, u32[]{:S(2)}, u32[]{:S(2)}) collective-permute-start(bf16[128,4,2,64]{0,3,2,1:T(8,128)(2,1)S(1)} %fusion.402), channel_id=1, source_target_pairs={{8,0},{16,8},{24,16},{9,1},{17,9},{25,17},{10,2},{18,10},{26,18},{... | collective-permute-start | bytes 393224 | tf_op jit(solution)/shard_map/while/body/eval_jaxpr/ppermute | solution.py:23
  230.8 7.1 %collective-permute-start.3 = (bf16[128,2,2,64]{0,3,2,1:T(8,128)(2,1)S(1)}, bf16[128,2,2,64]{0,3,2,1:T(8,128)(2,1)S(1)}, u32[]{:S(2)}, u32[]{:S(2)}) collective-permute-start(bf16[128,2,2,64]{0,3,2,1:T(8,128)(2,1)S(1)} %get-tuple-element.1001), channel_id=1, source_target_pairs={{1,0},{2,1},{3,2},{4,3},{5,4},{6,5},{7,6},{9,8},{10,9},{11,10},{12... | collective-permute-start | bytes 196616 | tf_op jit(solution)/shard_map/while/body/eval_jaxpr/ppermute | solution.py:15
  245.1 6.0 %collective-permute-start.5 = (bf16[128,4,2,64]{0,3,2,1:T(8,128)(2,1)S(1)}, bf16[128,4,2,64]{0,3,2,1:T(8,128)(2,1)S(1)}, u32[]{:S(2)}, u32[]{:S(2)}) collective-permute-start(bf16[128,4,2,64]{0,3,2,1:T(8,128)(2,1)S(1)} %fusion.402), channel_id=1, source_target_pairs={{8,0},{16,8},{24,16},{9,1},{17,9},{25,17},{10,2},{18,10},{26,18},{... | collective-permute-start | bytes 393224 | tf_op jit(solution)/shard_map/while/body/eval_jaxpr/ppermute | solution.py:23
  (59 other events, 122.0 us)
Sparse Core Ops, SparseCore 0:
  263.6 156.1 all-reduce.13
where the time goes:
time: 437 us; the launch traced here: 433 us
  waiting for transfers between devices  182 us (42%)
  starting transfers between devices  88.9 us (20%)
  local copies, waits for them, and re-layouts  69.6 us (16%)
  matrix products  43.5 us (10%)
  other arithmetic  20.1 us (5%)
  between operations  14.9 us (3%)
  blocking collectives  12 us (3%)
    psum x1, waiting for transfers between devices, on_device(): weight_total, bias_total = lax.psum((weight_terms, bias_terms), 'space')  144 us
    ppermute x10, starting transfers between devices, with_halo(): lax.ppermute(lax.slice_in_dim(block, 0, width, axis=dim), axis, backward)  34.6 us
    ppermute x10, starting transfers between devices, with_halo(): lax.ppermute(lax.slice_in_dim(block, block.shape[dim] - width, None, axis...  32.3 us
    unnamed x91, local copies, waits for them, and re-layouts  28.4 us
    ppermute x8, waiting for transfers between devices, passed_along(): return lax.ppermute(array, axis, pairs)  26.2 us
    dot_general x40, matrix products, convolve_rows(): jnp.einsum('ok,kxyz->oxyz', kernel[offset], stacked[:, offset:offset + co...  25.5 us
    ppermute x8, starting transfers between devices, passed_along(): return lax.ppermute(array, axis, pairs)  22 us
    while x216, local copies, waits for them, and re-layouts  19.6 us
  transfers between devices with their start and end apart: 29, of which 22 were waited for; matrix products, arithmetic and copies ran while one was open for 7% of the time, Pallas kernels for 0%

commit v1 on v0

v1 whole, which is shorter than its diff:
```python
import functools

import jax
import jax.numpy as jnp
from jax import lax
from jax.experimental import pallas as pl
from jax.experimental.pallas import tpu as pltpu
from jax.sharding import PartitionSpec as P

F32 = jnp.float32
BF16 = jnp.bfloat16


def silu_slope(pre, logistic):
    return logistic * (1.0 + pre * (1.0 - logistic))


def kernel(
    dims,
    x_ref, up_ref, cot_ref, w_ref, bias_ref,
    eg_ref, ug_ref, wg_ref, bg_ref,
    wf, wa, xw, dw, gd, ge, uw, patx, path, patt, s1, s2, sg, fg,
    part, ra, csum, rb, fin,
    send_sem, recv_sem, a_send, a_recv, b_send, b_recv, c_send, c_recv, d_send, d_recv,
):
    S, n, R, Z, Y, C = dims
    F = Y * C
    nz = n // 2
    chunk = csum.shape[1] // nz
    bias_row = 27 * C
    sec = lax.axis_index("section")
    p = lax.axis_index("space")
    core = lax.rem(p, 2)
    chip = lax.div(p, 2)
    partner = p + 1 - 2 * core

    def rows(first, count):
        return pl.ds(first * Z, count * Z)

    def dev(s, q):
        return {"section": s, "space": q}

    def copy(src, dst, ssem, rsem, where):
        return pltpu.make_async_remote_copy(
            src_ref=src, dst_ref=dst, send_sem=ssem, recv_sem=rsem,
            device_id=where, device_id_type=pl.DeviceIdType.MESH,
        )

    has_left, has_right = p > 0, p < n - 1

    for buf in (xw, dw):
        buf[rows(0, R), :] = jnp.zeros((R * Z, F), BF16)
        buf[rows(2 * R, R), :] = jnp.zeros((R * Z, F), BF16)
    for buf in (gd, ge, uw):
        buf[...] = jnp.zeros(buf.shape, BF16)

    barrier = pltpu.get_barrier_semaphore()
    for q in range(n):
        @pl.when(q != p)
        def _():
            pl.semaphore_signal(barrier, inc=1, device_id=dev(sec, q),
                                device_id_type=pl.DeviceIdType.MESH)
    for ds in (-1, 1):
        for dp in (-1, 0, 1):
            ok = (sec + ds >= 0) & (sec + ds < S) & (p + dp >= 0) & (p + dp < n)

            @pl.when(ok)
            def _():
                pl.semaphore_signal(barrier, inc=1, device_id=dev(sec + ds, p + dp),
                                    device_id_type=pl.DeviceIdType.MESH)
    sides = jnp.where(sec > 0, 1, 0) + jnp.where(sec < S - 1, 1, 0)
    wide = 1 + jnp.where(has_left, 1, 0) + jnp.where(has_right, 1, 0)
    pl.semaphore_wait(barrier, n - 1 + sides * wide)

    def spread(srcs, dsts, sids, rids, target, also=True, mid=None):
        left = (also & has_left, lambda: copy(
            srcs[0], dsts[1], send_sem.at[sids[0]], recv_sem.at[rids[1]], dev(target, p - 1)))
        right = (also & has_right, lambda: copy(
            srcs[1], dsts[0], send_sem.at[sids[1]], recv_sem.at[rids[0]], dev(target, p + 1)))
        out = [left, right]
        if mid is not None:
            out.append((also, lambda: copy(
                mid[0], mid[1], send_sem.at[sids[2]], recv_sem.at[rids[2]], dev(target, p))))
        return out

    pending = []

    def start(copies):
        for ok, make in copies:
            @pl.when(ok)
            def _():
                make().start()
        pending.extend(copies)

    def arrive(dst, rid, ok):
        @pl.when(ok)
        def _():
            copy(dst, dst, send_sem.at[rid], recv_sem.at[rid], dev(sec, partner)).wait_recv()

    start(spread((x_ref, x_ref), (xw.at[rows(0, R)], xw.at[rows(2 * R, R)]), (0, 1), (0, 1), sec))
    start(spread((cot_ref.at[rows(0, 2)], cot_ref.at[rows(R - 2, 2)]),
                 (gd.at[rows(0, 2)], gd.at[rows(R + 2, 2)]), (4, 5), (4, 5), sec, also=sec == 0))

    xw[rows(R, R), :] = x_ref[...]

    @pl.when(sec == 0)
    def _():
        gd[rows(2, R), :] = cot_ref[...]

    def build(step, carry):
        l, a = lax.div(step, 3), lax.rem(step, 3)
        for y in range(Y):
            for v in range(Y):
                b = v - y + 1
                for c in range(3):
                    if 0 <= b <= 2:
                        lane = (3 * b + c) * C
                        tap = w_ref[l, a, :, lane:lane + C]
                    else:
                        tap = jnp.zeros((C, C), BF16)
                    wf[l, a, y * C:(y + 1) * C, c * F + v * C:c * F + (v + 1) * C] = tap
                    wa[l, 2 - a, (2 - c) * F + y * C:(2 - c) * F + (y + 1) * C, v * C:(v + 1) * C] = tap
        return carry

    lax.fori_loop(0, w_ref.shape[0] * 3, build, 0)

    def patches(value, pat):
        count = value.shape[0]
        wide_value = value.astype(F32)
        depth = lax.rem(lax.broadcasted_iota(jnp.int32, (count, F), 0), Z)
        low = jnp.where(depth == 0, 0.0, pltpu.roll(wide_value, 1, 0))
        high = jnp.where(depth == Z - 1, 0.0, pltpu.roll(wide_value, count - 1, 0))
        pat[0:count, 0:F] = low.astype(BF16)
        pat[0:count, F:2 * F] = value
        pat[0:count, 2 * F:3 * F] = high.astype(BF16)

    def conv(pat, l, count):
        total = None
        for a in range(3):
            term = lax.dot_general(
                pat[rows(a, count), :], wf[l, a], (((1,), (1,)), ((), ())),
                preferred_element_type=F32)
            total = term if total is None else total + term
        return total

    def conv_back(pat, l, count):
        total = None
        for a in range(3):
            term = jnp.dot(pat[rows(a, count), :], wa[l, a], preferred_element_type=F32)
            total = term if total is None else total + term
        return total

    def inside(count, margin):
        position = lax.div(lax.broadcasted_iota(jnp.int32, (count * Z, F), 0), Z) + p * R - margin
        return (position >= 0) & (position < n * R)

    def bias_of(l):
        one = bias_ref[l:l + 1, :]
        return jnp.concatenate([one] * Y, axis=1)

    def forward(blk, field):
        patches(field, patx.at[blk])
        first = conv(patx.at[blk], 2 * blk, R + 6) + bias_of(2 * blk)
        logistic = jax.nn.sigmoid(first)
        act = jnp.where(inside(R + 6, 3), first * logistic, 0.0).astype(BF16)
        slope = jnp.where(inside(R + 6, 3), silu_slope(first, logistic), 0.0)
        s1[blk] = slope[2 * Z:(R + 4) * Z, :]
        patches(act, path.at[blk])
        second = conv(path.at[blk], 2 * blk + 1, R + 4) + bias_of(2 * blk + 1)
        logistic = jax.nn.sigmoid(second)
        s2[blk] = silu_slope(second, logistic)
        return (second * logistic)[2 * Z:(R + 2) * Z, :].astype(BF16)

    arrive(xw.at[rows(0, R)], 0, has_left)
    arrive(xw.at[rows(2 * R, R)], 1, has_right)
    enc_out = forward(0, xw[...])
    dw[rows(R, R), :] = (enc_out.astype(F32) + up_ref[...].astype(F32)).astype(BF16)
    start(spread((dw.at[rows(R, R)], dw.at[rows(R, R)]),
                 (dw.at[rows(0, R)], dw.at[rows(2 * R, R)]), (2, 3), (2, 3), sec))
    arrive(dw.at[rows(0, R)], 2, has_left)
    arrive(dw.at[rows(2 * R, R)], 3, has_right)
    forward(1, dw[...])

    def backward(blk, cotangent, out_ref):
        second = (cotangent * s2[blk]).astype(BF16)
        sg[blk] = second
        patches(second, patt)
        hidden = conv_back(patt, 2 * blk + 1, R + 2)
        first = (hidden * s1[blk]).astype(BF16)
        fg[blk] = first
        patches(first, patt)
        out_ref[...] = conv_back(patt, 2 * blk, R).astype(BF16)

    def weight_part(blk, layer, grads, pat, offset):
        summed = jnp.sum(grads.astype(F32), axis=0, keepdims=True)
        bias = sum(summed[:, y * C:(y + 1) * C] for y in range(Y))
        extra = csum.shape[1] - bias_row
        part[blk, layer, bias_row:bias_row + extra, :] = jnp.broadcast_to(bias, (extra, C)).astype(BF16)
        turned = grads.astype(F32).T.astype(BF16)
        for a in range(3):
            grid = jnp.dot(turned, pat[rows(offset + a, R), :], preferred_element_type=F32)
            for b in range(3):
                for c in range(3):
                    acc = None
                    for y in range(Y):
                        v = y + b - 1
                        if 0 <= v < Y:
                            term = grid[y * C:(y + 1) * C, c * F + v * C:c * F + (v + 1) * C]
                            acc = term if acc is None else acc + term
                    row = (a * 9 + 3 * b + c) * C
                    part[blk, layer, row:row + C, :] = acc.astype(BF16)

    def stretch(t):
        return pl.ds(pl.multiple_of(t * chunk, 16), chunk)

    def other(j):
        return lax.rem(chip + j, nz)

    def copy_a(blk):
        return copy(part.at[blk, 1 - core], ra.at[blk], a_send.at[blk], a_recv.at[blk],
                    dev(sec, partner))

    def copy_b(blk, t):
        return copy(csum.at[blk, stretch(t)], rb.at[blk, chip], b_send.at[blk, t],
                    b_recv.at[blk, chip], dev(sec, 2 * t + core))

    def copy_c(blk, t):
        here = fin.at[blk, core, stretch(chip)]
        return copy(here, here, c_send.at[blk, t], c_recv.at[blk, chip], dev(sec, 2 * t + core))

    def copy_d(blk, t):
        here = fin.at[blk, core, stretch(t)]
        return copy(here, here, d_send.at[blk, t], d_recv.at[blk, t], dev(sec, partner))

    def reduce_begin(blk):
        weight_part(blk, 1, sg[blk, rows(2, R), :], path.at[blk], 2)
        weight_part(blk, 0, fg[blk, rows(1, R), :], patx.at[blk], R - 1)
        copy_a(blk).start()

    def reduce_pair(blk):
        copy_a(blk).wait_recv()
        csum[blk] = (part[blk, core].astype(F32) + ra[blk].astype(F32)).astype(BF16)
        for j in range(1, nz):
            copy_b(blk, other(j)).start()
        rb[blk, chip] = csum[blk, stretch(chip), :]

    def reduce_chips(blk):
        for j in range(1, nz):
            t = other(j)
            copy(csum.at[blk, stretch(t)], rb.at[blk, t], b_send.at[blk, t],
                 b_recv.at[blk, t], dev(sec, partner)).wait_recv()
        total = rb[blk, 0].astype(F32)
        for t in range(1, nz):
            total = total + rb[blk, t].astype(F32)
        fin[blk, core, stretch(chip), :] = total.astype(BF16)
        for j in range(1, nz):
            copy_c(blk, other(j)).start()
        copy_d(blk, chip).start()

    def gather(blk):
        for j in range(1, nz):
            t = other(j)
            there = fin.at[blk, core, stretch(t)]
            copy(there, there, c_send.at[blk, t], c_recv.at[blk, t], dev(sec, partner)).wait_recv()
            copy_d(blk, t).start()

    def finish(blk):
        for t in range(nz):
            there = fin.at[blk, 1 - core, stretch(t)]
            copy(there, there, d_send.at[blk, t], d_recv.at[blk, t], dev(sec, partner)).wait_recv()
        for layer in range(2):
            for a in range(3):
                for k in range(9):
                    row = (a * 9 + k) * C
                    wg_ref[2 * blk + layer, a, :, k * C:(k + 1) * C] = (
                        fin[blk, layer, row:row + C, :].astype(F32))
            bg_ref[2 * blk + layer:2 * blk + layer + 1, :] = (
                fin[blk, layer, bias_row:bias_row + 16, :].astype(F32)[0:1, :])

    def drain(blk):
        copy_a(blk).wait_send()
        copy_d(blk, chip).wait_send()
        for j in range(1, nz):
            copy_b(blk, other(j)).wait_send()
            copy_c(blk, other(j)).wait_send()
            copy_d(blk, other(j)).wait_send()

    later = sec > 0
    arrive(gd.at[rows(0, 2)], 4, has_left)
    arrive(gd.at[rows(R + 2, 2)], 5, has_right)
    arrive(gd.at[rows(2, R)], 6, later)
    backward(1, gd[...].astype(F32), ug_ref)
    start(spread((ug_ref.at[rows(0, 2)], ug_ref.at[rows(R - 2, 2)]),
                 (gd.at[rows(0, 2)], gd.at[rows(R + 2, 2)]), (6, 7, 8), (4, 5, 6), sec + 1,
                 also=sec < S - 1, mid=(ug_ref, gd.at[rows(2, R)])))
    start(spread((ug_ref.at[rows(0, 2)], ug_ref.at[rows(R - 2, 2)]),
                 (uw.at[rows(0, 2)], uw.at[rows(R + 2, 2)]), (9, 10), (7, 8), sec))
    uw[rows(2, R), :] = ug_ref[...]

    @pl.when(sec < S - 1)
    def _():
        reduce_begin(1)
        reduce_pair(1)

    @pl.when(sec < S - 2)
    def _():
        reduce_chips(1)

    above = sec < S - 1
    arrive(uw.at[rows(0, 2)], 7, has_left)
    arrive(uw.at[rows(R + 2, 2)], 8, has_right)
    arrive(ge.at[rows(0, 2)], 9, above & has_left)
    arrive(ge.at[rows(R + 2, 2)], 10, above & has_right)
    arrive(ge.at[rows(2, R)], 11, above)
    combined = (uw[...].astype(F32) + ge[...].astype(F32)).astype(BF16)
    backward(0, combined.astype(F32), eg_ref)
    start(spread((eg_ref.at[rows(0, 2)], eg_ref.at[rows(R - 2, 2)]),
                 (ge.at[rows(0, 2)], ge.at[rows(R + 2, 2)]), (11, 12, 13), (9, 10, 11), sec - 1,
                 also=sec > 0, mid=(eg_ref, ge.at[rows(2, R)])))

    @pl.when(sec == S - 1)
    def _():
        reduce_begin(1)
        reduce_pair(1)

    reduce_begin(0)
    reduce_pair(0)

    @pl.when(sec >= S - 2)
    def _():
        reduce_chips(1)

    gather(1)
    finish(1)
    reduce_chips(0)
    gather(0)
    finish(0)

    for ok, make in pending:
        @pl.when(ok)
        def _():
            make().wait_send()
    drain(1)
    drain(0)


def on_device(dims, encoder_inputs, upper_inputs, output_cotangent, weights, biases):
    S, n, R, Z, Y, C = dims
    F = Y * C
    nz = n // 2
    unit = 16 * nz
    height = -(-(27 * C + 16) // unit) * unit

    def cells(field):
        return field.transpose(1, 3, 2, 0).reshape(R * Z, F)

    def fields(value):
        return value.reshape(R, Z, Y, C).transpose(3, 0, 2, 1)

    block = jax.ShapeDtypeStruct((R * Z, F), BF16)
    dma = pltpu.SemaphoreType.DMA
    eg, ug, wg, bg = pl.pallas_call(
        functools.partial(kernel, dims),
        out_shape=(
            block, block,
            jax.ShapeDtypeStruct(weights.shape[1:], F32),
            jax.ShapeDtypeStruct(biases.shape[1:], F32),
        ),
        in_specs=[pl.BlockSpec(memory_space=pltpu.VMEM)] * 5,
        out_specs=tuple([pl.BlockSpec(memory_space=pltpu.VMEM)] * 4),
        scratch_shapes=[
            pltpu.VMEM((4, 3, F, 3 * F), BF16),
            pltpu.VMEM((4, 3, 3 * F, F), BF16),
            pltpu.VMEM((3 * R * Z, F), BF16),
            pltpu.VMEM((3 * R * Z, F), BF16),
            pltpu.VMEM(((R + 4) * Z, F), BF16),
            pltpu.VMEM(((R + 4) * Z, F), BF16),
            pltpu.VMEM(((R + 4) * Z, F), BF16),
            pltpu.VMEM((2, (R + 8) * Z, 3 * F), BF16),
            pltpu.VMEM((2, (R + 6) * Z, 3 * F), BF16),
            pltpu.VMEM(((R + 4) * Z, 3 * F), BF16),
            pltpu.VMEM((2, (R + 2) * Z, F), F32),
            pltpu.VMEM((2, (R + 4) * Z, F), F32),
            pltpu.VMEM((2, (R + 4) * Z, F), BF16),
            pltpu.VMEM((2, (R + 2) * Z, F), BF16),
            pltpu.VMEM((2, 2, height, C), BF16),
            pltpu.VMEM((2, height, C), BF16),
            pltpu.VMEM((2, height, C), BF16),
            pltpu.VMEM((2, nz, height // nz, C), BF16),
            pltpu.VMEM((2, 2, height, C), BF16),
            dma((14,)), dma((12,)),
            dma((2,)), dma((2,)),
            dma((2, nz)), dma((2, nz)),
            dma((2, nz)), dma((2, nz)),
            dma((2, nz)), dma((2, nz)),
        ],
        compiler_params=pltpu.CompilerParams(
            collective_id=0, has_side_effects=True, vmem_limit_bytes=58 * 1024 * 1024
        ),
    )(
        cells(encoder_inputs[0, 0]), cells(upper_inputs[0, 0]), cells(output_cotangent[0]),
        weights[0], biases[0],
    )
    return (fields(eg)[None, None], fields(ug)[None, None], wg[None], bg[None])


def solution(mesh):
    def run(encoder_inputs, upper_inputs, output_cotangent, weights, biases):
        channels, total, lateral, depth = encoder_inputs.shape[2:]
        n = mesh.shape["space"]
        dims = (mesh.shape["section"], n, total // n, depth, lateral, channels)
        return jax.shard_map(
            functools.partial(on_device, dims),
            mesh=mesh,
            in_specs=(
                P("section", None, None, "space", None, None),
                P("section", None, None, "space", None, None),
                P(None, None, "space", None, None),
                P("section", None, None, None, None),
                P("section", None, None),
            ),
            out_specs=(
                P("section", None, None, "space", None, None),
                P("section", None, None, "space", None, None),
                P("section", None, None, None, None),
                P("section", None, None),
            ),
            check_vma=False,
        )(encoder_inputs, upper_inputs, output_cotangent, weights, biases)

    return run
```

time: 437 us -> 169 us (0.39)
  waiting for transfers between devices: 182 us -> 0 us
  Pallas kernels: 0 us -> 153 us
  starting transfers between devices: 88.9 us -> 0 us
  local copies, waits for them, and re-layouts: 69.6 us -> 14.8 us
  matrix products: 43.5 us -> 0 us
  other arithmetic: 20.1 us -> 0 us
  between operations: 14.9 us -> 0.65 us
  blocking collectives: 12 us -> 0 us
    pallas_call x0 -> x1, Pallas kernels: none -> 153 us  [on_device(): pl.pallas_call(functools.partial(kernel, dims), out_shape=(block, block,...]
    psum x1 -> x0, waiting for transfers between devices: 144 us -> none  [on_device(): weight_total, bias_total = lax.psum((weight_terms, bias_terms), 'space')]
    ppermute x28 -> x0, starting transfers between devices: 88.9 us -> none  [the longest x10 34.6 us: with_halo(): lax.ppermute(lax.slice_in_dim(block, 0, width, axis=dim), axis, backward)]
    dot_general x72 -> x0, matrix products: 43.5 us -> none  [the longest x40 25.5 us: convolve_rows(): jnp.einsum('ok,kxyz->oxyz', kernel[offset], stacked[:, offset:offset + co...]
    ppermute x28 -> x0, waiting for transfers between devices: 37.8 us -> none  [the longest x8 26.2 us: passed_along(): return lax.ppermute(array, axis, pairs)]
    unnamed x91 -> x5, local copies, waits for them, and re-layouts: 28.4 us -> 7.68 us
    while x216 -> x0, local copies, waits for them, and re-layouts: 19.6 us -> none
    psum x1 -> x0, blocking collectives: 12 us -> none  [on_device(): weight_total, bias_total = lax.psum((weight_terms, bias_terms), 'space')]
  transfers between devices with their start and end apart: 29 -> 0, of which waited for: 22 -> 0; matrix products, arithmetic and copies ran while one was open for 7% -> 0% of each run, Pallas kernels for 0% -> 0%
where the time goes in v1:
time: 169 us
  Pallas kernels  153 us (91%)
  local copies, waits for them, and re-layouts  14.8 us (9%)
    pallas_call x1, Pallas kernels, on_device(): pl.pallas_call(functools.partial(kernel, dims), out_shape=(block, block,...  153 us
    unnamed x5, local copies, waits for them, and re-layouts  7.68 us

profile of v1, /device:TPU:23, one launch (start us, length us, event | category | flops | bytes accessed | tf_op | source)
XLA Modules:
  0.0 168.7 jit_solution(12116572313671931222)
XLA Ops:
  0.6 1.0 copy.9
  1.7 0.7 copy.22
  2.3 1.0 copy.10
  3.4 1.0 copy.11
  4.4 0.7 copy_bitcast_fusion
  5.2 153.3 %shard_map.84 = (bf16[256,256]{1,0:T(8,128)(2,1)}, bf16[256,256]{1,0:T(8,128)(2,1)}, f32[4,3,128,1152]{3,2,1,0:T(8,128)}, f32[4,128]{1,0:T(4,128)}) custom-call(bf16[256,256]{1,0:T(8,128)(2,1)} %bitcast.38, bf16[256,256]{1,0:T(8,128)(2,1)} %get-tuple-element.13.up_ref, bf16[256,256]{1,0:T(8,128)(2,1)} %get-tuple-element.12.cot_ref, ...), custom_call_target="tpu_custom_call" | custom-call | tf_op jit(solution)/shard_map/pallas_call | solution.py:362
  158.5 0.9 reshape.26
  159.4 0.7 copy.24
  160.1 0.9 reshape.27
  161.0 0.7 copy.23
  161.7 0.0 copy-start
  161.7 6.4 %copy.27 = f32[1,4,3,128,1152]{4,3,2,1,0:T(8,128)} copy(f32[1,4,3,128,1152]{4,3,2,1,0:T(8,128)} %bitcast.36) | data formatting | bytes 14155776
  168.1 0.0 copy-done
  168.1 0.6 copy.28
Async XLA Ops:
  161.7 6.4 %copy-start = (f32[4,128]{1,0:T(4,128)S(1)}, f32[4,128]{1,0:T(4,128)}, u32[]{:S(2)}) copy-start(f32[4,128]{1,0:T(4,128)} %get-tuple-element.11) | copy-start | bytes 6148

commit v2 on v1

--- a/solution.py
+++ b/solution.py
@@ -18,15 +18,17 @@
 def kernel(
     dims,
     x_ref, up_ref, cot_ref, w_ref, bias_ref,
-    eg_ref, ug_ref, wg_ref, bg_ref,
+    eg_ref, ug_ref, fin,
     wf, wa, xw, dw, gd, ge, uw, patx, path, patt, s1, s2, sg, fg,
-    part, ra, csum, rb, fin,
+    part, ra, csum, rb,
     send_sem, recv_sem, a_send, a_recv, b_send, b_recv, c_send, c_recv, d_send, d_recv,
 ):
     S, n, R, Z, Y, C = dims
     F = Y * C
     nz = n // 2
-    chunk = csum.shape[1] // nz
+    half = csum.shape[1] // 2
+    pieces = b_send.shape[2]
+    chunk = half // pieces
     bias_row = 27 * C
     sec = lax.axis_index("section")
     p = lax.axis_index("space")
@@ -210,27 +212,29 @@
                     row = (a * 9 + 3 * b + c) * C
                     part[blk, layer, row:row + C, :] = acc.astype(BF16)
 
-    def stretch(t):
-        return pl.ds(pl.multiple_of(t * chunk, 16), chunk)
-
-    def other(j):
-        return lax.rem(chip + j, nz)
+    def stretch(side, i):
+        return pl.ds(pl.multiple_of(side * half + i * chunk, 16), chunk)
+
+    ends = (chip == 0, chip == nz - 1)
+
+    def onward(side):
+        return dev(sec, p + (4 * side - 2))
 
     def copy_a(blk):
         return copy(part.at[blk, 1 - core], ra.at[blk], a_send.at[blk], a_recv.at[blk],
                     dev(sec, partner))
 
-    def copy_b(blk, t):
-        return copy(csum.at[blk, stretch(t)], rb.at[blk, chip], b_send.at[blk, t],
-                    b_recv.at[blk, chip], dev(sec, 2 * t + core))
-
-    def copy_c(blk, t):
-        here = fin.at[blk, core, stretch(chip)]
-        return copy(here, here, c_send.at[blk, t], c_recv.at[blk, chip], dev(sec, 2 * t + core))
-
-    def copy_d(blk, t):
-        here = fin.at[blk, core, stretch(t)]
-        return copy(here, here, d_send.at[blk, t], d_recv.at[blk, t], dev(sec, partner))
+    def copy_b(blk, side, i):
+        return copy(csum.at[blk, stretch(side, i)], rb.at[blk, stretch(side, i)],
+                    b_send.at[blk, side, i], b_recv.at[blk, side, i], onward(side))
+
+    def copy_c(blk, side, i):
+        here = fin.at[blk, core, stretch(side, i)]
+        return copy(here, here, c_send.at[blk, side, i], c_recv.at[blk, side, i], onward(1 - side))
+
+    def copy_d(blk, side, i, layer):
+        here = fin.at[blk, layer, stretch(side, i)]
+        return copy(here, here, d_send.at[blk, side, i], d_recv.at[blk, side, i], dev(sec, partner))
 
     def reduce_begin(blk):
         weight_part(blk, 1, sg[blk, rows(2, R), :], path.at[blk], 2)
@@ -240,50 +244,68 @@
     def reduce_pair(blk):
         copy_a(blk).wait_recv()
         csum[blk] = (part[blk, core].astype(F32) + ra[blk].astype(F32)).astype(BF16)
-        for j in range(1, nz):
-            copy_b(blk, other(j)).start()
-        rb[blk, chip] = csum[blk, stretch(chip), :]
-
-    def reduce_chips(blk):
-        for j in range(1, nz):
-            t = other(j)
-            copy(csum.at[blk, stretch(t)], rb.at[blk, t], b_send.at[blk, t],
-                 b_recv.at[blk, t], dev(sec, partner)).wait_recv()
-        total = rb[blk, 0].astype(F32)
-        for t in range(1, nz):
-            total = total + rb[blk, t].astype(F32)
-        fin[blk, core, stretch(chip), :] = total.astype(BF16)
-        for j in range(1, nz):
-            copy_c(blk, other(j)).start()
-        copy_d(blk, chip).start()
-
-    def gather(blk):
-        for j in range(1, nz):
-            t = other(j)
-            there = fin.at[blk, core, stretch(t)]
-            copy(there, there, c_send.at[blk, t], c_recv.at[blk, t], dev(sec, partner)).wait_recv()
-            copy_d(blk, t).start()
-
-    def finish(blk):
-        for t in range(nz):
-            there = fin.at[blk, 1 - core, stretch(t)]
-            copy(there, there, d_send.at[blk, t], d_recv.at[blk, t], dev(sec, partner)).wait_recv()
-        for layer in range(2):
-            for a in range(3):
-                for k in range(9):
-                    row = (a * 9 + k) * C
-                    wg_ref[2 * blk + layer, a, :, k * C:(k + 1) * C] = (
-                        fin[blk, layer, row:row + C, :].astype(F32))
-            bg_ref[2 * blk + layer:2 * blk + layer + 1, :] = (
-                fin[blk, layer, bias_row:bias_row + 16, :].astype(F32)[0:1, :])
-
-    def drain(blk):
-        copy_a(blk).wait_send()
-        copy_d(blk, chip).wait_send()
-        for j in range(1, nz):
-            copy_b(blk, other(j)).wait_send()
-            copy_c(blk, other(j)).wait_send()
-            copy_d(blk, other(j)).wait_send()
+        each(lambda i: begin_line(blk, i))
+
+    def begin_line(blk, i):
+        for side in range(2):
+            @pl.when(ends[1 - side])
+            def _():
+                copy_b(blk, side, i).start()
+
+    def line_step(blk, t):
+        for side in range(2):
+            hops = chip if side == 1 else nz - 1 - chip
+            i = t - hops
+
+            @pl.when((i >= 0) & (i < pieces) & ~ends[1 - side])
+            def _():
+                copy_b(blk, side, i).wait_recv()
+                here = stretch(side, i)
+                total = (csum[blk, here, :].astype(F32) + rb[blk, here, :].astype(F32)).astype(BF16)
+
+                @pl.when(~ends[side])
+                def _():
+                    csum[blk, here, :] = total
+                    copy_b(blk, side, i).start()
+
+                @pl.when(ends[side])
+                def _():
+                    fin[blk, core, here, :] = total
+                    copy_c(blk, side, i).start()
+                    copy_d(blk, side, i, core).start()
+        for side in range(2):
+            hops = chip if side == 1 else nz - 1 - chip
+            i = t - 2 * (nz - 1) + hops
+
+            @pl.when((i >= 0) & (i < pieces) & ~ends[side])
+            def _():
+                copy_c(blk, side, i).wait_recv()
+
+                @pl.when(~ends[1 - side])
+                def _():
+                    copy_c(blk, side, i).start()
+                copy_d(blk, side, i, core).start()
+
+    span = pieces + 2 * (nz - 1)
+
+    def drain_step(blk, i):
+        for side in range(2):
+            copy_d(blk, side, i, 1 - core).wait_recv()
+            copy_d(blk, side, i, core).wait_send()
+
+            @pl.when(~ends[side])
+            def _():
+                copy_b(blk, side, i).wait_send()
+
+            @pl.when(~ends[1 - side])
+            def _():
+                copy_c(blk, side, i).wait_send()
+
+    def each(step, count=None):
+        def body(i, carry):
+            step(i)
+            return carry
+        lax.fori_loop(0, pieces if count is None else count, body, 0)
 
     later = sec > 0
     arrive(gd.at[rows(0, 2)], 4, has_left)
@@ -304,7 +326,7 @@
 
     @pl.when(sec < S - 2)
     def _():
-        reduce_chips(1)
+        each(lambda t: line_step(1, t), span)
 
     above = sec < S - 1
     arrive(uw.at[rows(0, 2)], 7, has_left)
@@ -328,27 +350,38 @@
 
     @pl.when(sec >= S - 2)
     def _():
-        reduce_chips(1)
-
-    gather(1)
-    finish(1)
-    reduce_chips(0)
-    gather(0)
-    finish(0)
+        def both(t):
+            line_step(1, t)
+            line_step(0, t - pieces)
+        each(both, span + pieces)
+
+    @pl.when(sec < S - 2)
+    def _():
+        each(lambda t: line_step(0, t), span)
 
     for ok, make in pending:
         @pl.when(ok)
         def _():
             make().wait_send()
-    drain(1)
-    drain(0)
+    for blk in range(2):
+        copy_a(blk).wait_send()
+        each(lambda i: drain_step(blk, i))
+
+
+def spread_out(fin_ref, out_ref):
+    C = fin_ref.shape[3]
+    taps = out_ref.shape[3] // C
+    for a in range(3):
+        for k in range(taps):
+            row = (a * taps + k) * C
+            out_ref[0, a, :, k * C:(k + 1) * C] = fin_ref[0, 0, row:row + C, :].astype(F32)
 
 
 def on_device(dims, encoder_inputs, upper_inputs, output_cotangent, weights, biases):
     S, n, R, Z, Y, C = dims
     F = Y * C
-    nz = n // 2
-    unit = 16 * nz
+    pieces = 7
+    unit = 32 * pieces
     height = -(-(27 * C + 16) // unit) * unit
 
     def cells(field):
@@ -359,15 +392,14 @@
 
     block = jax.ShapeDtypeStruct((R * Z, F), BF16)
     dma = pltpu.SemaphoreType.DMA
-    eg, ug, wg, bg = pl.pallas_call(
+    eg, ug, total = pl.pallas_call(
         functools.partial(kernel, dims),
         out_shape=(
             block, block,
-            jax.ShapeDtypeStruct(weights.shape[1:], F32),
-            jax.ShapeDtypeStruct(biases.shape[1:], F32),
+            jax.ShapeDtypeStruct((2, 2, height, C), BF16),
         ),
         in_specs=[pl.BlockSpec(memory_space=pltpu.VMEM)] * 5,
-        out_specs=tuple([pl.BlockSpec(memory_space=pltpu.VMEM)] * 4),
+        out_specs=tuple([pl.BlockSpec(memory_space=pltpu.VMEM)] * 3),
         scratch_shapes=[
             pltpu.VMEM((4, 3, F, 3 * F), BF16),
             pltpu.VMEM((4, 3, 3 * F, F), BF16),
@@ -386,13 +418,12 @@
             pltpu.VMEM((2, 2, height, C), BF16),
             pltpu.VMEM((2, height, C), BF16),
             pltpu.VMEM((2, height, C), BF16),
-            pltpu.VMEM((2, nz, height // nz, C), BF16),
-            pltpu.VMEM((2, 2, height, C), BF16),
+            pltpu.VMEM((2, height, C), BF16),
             dma((14,)), dma((12,)),
             dma((2,)), dma((2,)),
-            dma((2, nz)), dma((2, nz)),
-            dma((2, nz)), dma((2, nz)),
-            dma((2, nz)), dma((2, nz)),
+            dma((2, 2, pieces)), dma((2, 2, pieces)),
+            dma((2, 2, pieces)), dma((2, 2, pieces)),
+            dma((2, 2, pieces)), dma((2, 2, pieces)),
         ],
         compiler_params=pltpu.CompilerParams(
             collective_id=0, has_side_effects=True, vmem_limit_bytes=58 * 1024 * 1024
@@ -401,6 +432,15 @@
         cells(encoder_inputs[0, 0]), cells(upper_inputs[0, 0]), cells(output_cotangent[0]),
         weights[0], biases[0],
     )
+    wg = pl.pallas_call(
+        spread_out,
+        grid=(2, 2),
+        out_shape=jax.ShapeDtypeStruct(weights.shape[1:], F32),
+        in_specs=[pl.BlockSpec((1, 1, 27 * C, C), lambda i, j: (i, j, 0, 0))],
+        out_specs=pl.BlockSpec((1,) + weights.shape[2:], lambda i, j: (2 * i + j, 0, 0, 0)),
+        compiler_params=pltpu.CompilerParams(vmem_limit_bytes=16 * 1024 * 1024),
+    )(total)
+    bg = total[:, :, 27 * C, :].reshape(4, C).astype(F32)
     return (fields(eg)[None, None], fields(ug)[None, None], wg[None], bg[None])
 
 

time: 169 us -> 145 us (0.86)
  the two profiles are of different devices: /device:TPU:23 before, /device:TPU:7 now
where the time goes in v2:
time: 145 us; the launch traced here: 144 us
  Pallas kernels  133 us (92%)
  local copies, waits for them, and re-layouts  9.8 us (7%)
    pallas_call x1, Pallas kernels, on_device(): pl.pallas_call(functools.partial(kernel, dims), out_shape=(block, block,...  130 us
    reshape x4, local copies, waits for them, and re-layouts, fields(): return value.reshape(R, Z, Y, C).transpose(3, 0, 2, 1)  3.23 us
    pallas_call x1, Pallas kernels, on_device(): pl.pallas_call(spread_out, grid=(2, 2), out_shape=jax.ShapeDtypeStruct(we...  3.22 us
    transpose x3, local copies, waits for them, and re-layouts, cells(): return field.transpose(1, 3, 2, 0).reshape(R * Z, F)  3.12 us

profile of v2, /device:TPU:7, one launch (start us, length us, event | category | flops | bytes accessed | tf_op | source)
XLA Modules:
  0.0 144.5 jit_solution(6166153600816085092)
XLA Ops:
  0.6 1.0 copy.9
  1.7 0.7 copy.22
  2.3 1.0 copy.10
  3.4 1.0 copy.11
  4.4 0.7 copy_bitcast_fusion
  5.2 129.5 %shard_map.84 = (bf16[256,256]{1,0:T(8,128)(2,1)}, bf16[256,256]{1,0:T(8,128)(2,1)}, bf16[2,2,3584,128]{3,2,1,0:T(8,128)(2,1)}) custom-call(bf16[256,256]{1,0:T(8,128)(2,1)} %bitcast.38, bf16[256,256]{1,0:T(8,128)(2,1)} %get-tuple-element.11.up_ref, bf16[256,256]{1,0:T(8,128)(2,1)} %get-tuple-element.10.cot_ref, bf16[4,3,128,1152]{3,2,1,0:T(8,128)(2,1)} %bitcast.37, ...), custom_call_target="tpu_custom_call" | custom-call | tf_op jit(solution)/shard_map/pallas_call | solution.py:395
  134.7 0.9 reshape.38
  135.6 0.7 copy.24
  136.3 1.3 slice_convert_fusion
  137.6 0.9 reshape.39
  138.5 0.7 copy.23
  139.2 0.0 copy-start
  139.2 2.0 %copy-done = bf16[2,2,3584,128]{3,2,1,0:T(8,128)(2,1)S(1)} copy-done((bf16[2,2,3584,128]{3,2,1,0:T(8,128)(2,1)S(1)}, bf16[2,2,3584,128]{3,2,1,0:T(8,128)(2,1)}, u32[]{:S(2)}) %copy-start) | copy-done | bytes 3670040
  141.2 3.2 %shard_map.85 = f32[4,3,128,1152]{3,2,1,0:T(8,128)} custom-call(bf16[2,2,3584,128]{3,2,1,0:T(8,128)(2,1)S(1)} %copy-done), custom_call_target="tpu_custom_call" | custom-call | tf_op jit(solution)/shard_map/pallas_call | solution.py:435
Async XLA Ops:
  139.2 2.0 %copy-start = (bf16[2,2,3584,128]{3,2,1,0:T(8,128)(2,1)S(1)}, bf16[2,2,3584,128]{3,2,1,0:T(8,128)(2,1)}, u32[]{:S(2)}) copy-start(bf16[2,2,3584,128]{3,2,1,0:T(8,128)(2,1)} %get-tuple-element.9.fin_ref) | copy-start | bytes 11010052
